TPU v7x, 32 devices: a whole 2x2x4 slice. The times are simulated.
32 devices in a mesh: dp: 16 (over z, y, x), tensor: 2 (over core).
Axes of the slice: x: 2, y: 2, z: 4, core: 2. Of those that a mesh axis runs over, the one named last changes fastest.
Arguments:
- tokens: bfloat16 [16384, 768], P(('dp', 'tensor')), may hold values from -6 to 6
- lengths: int32 [16], P('dp'), may hold values from 1 to 1024, 10240 in all
- qkv_weight: bfloat16 [3, 768, 768], P(None, 'dp', 'tensor'), may hold values from -0.21875 to 0.21875
- qv_bias: float32 [2, 768], P(None, 'tensor'), may hold values from -3 to 3
- out_weight: bfloat16 [768, 768], P('tensor', 'dp'), may hold values from -0.875 to 0.875
- out_bias: float32 [768], replicated, may hold values from -3 to 3
- up_weight: bfloat16 [768, 3072], P('dp', 'tensor'), may hold values from -0.21875 to 0.21875
- up_bias: float32 [3072], P('tensor'), may hold values from -3 to 3
- down_weight: bfloat16 [3072, 768], P('tensor', 'dp'), may hold values from -0.109375 to 0.109375
- down_bias: float32 [768], replicated, may hold values from -3 to 3
- norm1_gain: float32 [768], replicated, may hold values from 0.5 to 1.5
- norm1_shift: float32 [768], replicated, may hold values from -3 to 3
- norm2_gain: float32 [768], replicated, may hold values from 0.5 to 1.5
- norm2_shift: float32 [768], replicated, may hold values from -3 to 3
- cotangent: bfloat16 [16384, 768], P(('dp', 'tensor')), may hold values from -6 to 6
Outputs:
- layer_output: bfloat16 [16384, 768], P(('dp', 'tensor'))
- input_grad: bfloat16 [16384, 768], P(('dp', 'tensor'))
- grad_qkv_weight: float32 [3, 768, 768], P(None, 'dp', 'tensor')
- grad_qv_bias: float32 [2, 768], P(None, 'tensor')
- grad_out_weight: float32 [768, 768], P('tensor', 'dp')
- grad_out_bias: float32 [768], replicated
- grad_up_weight: float32 [768, 3072], P('dp', 'tensor')
- grad_up_bias: float32 [3072], P('tensor')
- grad_down_weight: float32 [3072, 768], P('tensor', 'dp')
- grad_down_bias: float32 [768], replicated
- grad_norm1_gain: float32 [768], replicated
- grad_norm1_shift: float32 [768], replicated
- grad_norm2_gain: float32 [768], replicated
- grad_norm2_shift: float32 [768], replicated
Inputs may be any that keep to these rules, and one draw needn't show every extreme that they name: lengths[s] is the count of real tokens of sequence s; some sequence has 1024.
All inputs are finite; a program needn't handle non-finite values. No bound on the sum of `lengths` on one device may be relied on, other than what follows from the above.
Results may differ from a plain program's by a relative error of at most 0.017.
Values may be sent and summed in bfloat16 or wider, within the bound.
A program may use at most 192 MiB of HBM per device.

v0:
```python
import jax
import jax.numpy as jnp
from jax import lax
from jax.sharding import PartitionSpec as P

HEAD_DIM = 64
LENGTH = 1024
EPSILON = 1e-05
NEGATIVE = -1e30


def layer_norm(values, norm_gain, norm_shift):
    center = values - jnp.mean(values, axis=-1, keepdims=True)
    spread = jnp.mean(center * center, axis=-1, keepdims=True)
    return center * lax.rsqrt(spread + EPSILON) * norm_gain + norm_shift


def gelu_exact(values):
    return jax.nn.gelu(values, approximate=False)


def matmul(left, right):
    return jnp.dot(left, right, preferred_element_type=jnp.float32)


def contract_rows(left, right):
    return lax.dot_general(
        left, right, (((0,), (0,)), ((), ())), preferred_element_type=jnp.float32
    )


def contract_cols(left, right):
    return lax.dot_general(
        left, right, (((1,), (1,)), ((), ())), preferred_element_type=jnp.float32
    )


def per_device(
    tokens,
    lengths,
    qkv_weight,
    qv_bias,
    out_weight,
    out_bias,
    up_weight,
    up_bias,
    down_weight,
    down_bias,
    norm1_gain,
    norm1_shift,
    norm2_gain,
    norm2_shift,
    cotangent,
):
    tok_rows = tokens.shape[0]
    local_width = qkv_weight.shape[2]
    head_count = local_width // HEAD_DIM
    seq_count = lengths.shape[0]
    block_rows = min(512, LENGTH)
    scaling = HEAD_DIM ** (-0.5)
    positions = jnp.arange(LENGTH)
    qkv_full, out_full, up_full, down_full = (
        lax.all_gather(qkv_weight, "dp", axis=1, tiled=True),
        lax.all_gather(out_weight, "dp", axis=1, tiled=True),
        lax.all_gather(up_weight, "dp", axis=0, tiled=True),
        lax.all_gather(down_weight, "dp", axis=1, tiled=True),
    )
    gathered = lax.all_gather(tokens, "tensor", axis=0, tiled=True)
    queries = (matmul(gathered, qkv_full[0]) + qv_bias[0]).astype(jnp.bfloat16)
    key_rows = matmul(gathered, qkv_full[1]).astype(jnp.bfloat16)
    value_rows = (matmul(gathered, qkv_full[2]) + qv_bias[1]).astype(jnp.bfloat16)

    def forward_seq(packed):
        seq_queries, seq_keys, seq_values, length = packed
        query_heads = seq_queries.reshape(LENGTH, head_count, HEAD_DIM)
        key_heads = seq_keys.reshape(LENGTH, head_count, HEAD_DIM)
        value_heads = seq_values.reshape(LENGTH, head_count, HEAD_DIM)
        usable = (positions < length)[None, None, :]
        context_blocks = []
        total_blocks = []
        for block_start in range(0, LENGTH, block_rows):
            block_q = query_heads[block_start : block_start + block_rows]
            scores = (
                jnp.einsum("qhd,khd->hqk", block_q, key_heads, preferred_element_type=jnp.float32)
                * scaling
            )
            scores = jnp.where(usable, scores, NEGATIVE)
            row_top = jnp.max(scores, axis=-1, keepdims=True)
            exponent = jnp.exp(scores - row_top)
            row_total = jnp.sum(exponent, axis=-1, keepdims=True)
            weights = (exponent / row_total).astype(jnp.bfloat16)
            block_context = jnp.einsum(
                "hqk,khd->qhd", weights, value_heads, preferred_element_type=jnp.float32
            )
            context_blocks.append(block_context.reshape(block_rows, local_width))
            total_blocks.append((row_top + jnp.log(row_total))[..., 0])
        return (
            jnp.concatenate(context_blocks, axis=0).astype(jnp.bfloat16),
            jnp.concatenate(total_blocks, axis=1),
        )

    shaped = (
        queries.reshape(seq_count, LENGTH, local_width),
        key_rows.reshape(seq_count, LENGTH, local_width),
        value_rows.reshape(seq_count, LENGTH, local_width),
    )
    contexts, log_totals = lax.map(forward_seq, (shaped[0], shaped[1], shaped[2], lengths))
    context_flat = contexts.reshape(seq_count * LENGTH, local_width)
    row_block = lax.slice_in_dim(context_flat, 0, tok_rows * lax.axis_size("tensor"), axis=0)
    attn = (
        lax.psum_scatter(matmul(row_block, out_full), "tensor", scatter_dimension=0, tiled=True)
        + out_bias
    )
    first_sum = tokens.astype(jnp.float32) + attn
    hidden = layer_norm(first_sum, norm1_gain, norm1_shift)
    hidden_low = hidden.astype(jnp.bfloat16)
    hidden_all = lax.all_gather(hidden_low, "tensor", axis=0, tiled=True)
    upper = matmul(hidden_all, up_full) + up_bias
    active = gelu_exact(upper).astype(jnp.bfloat16)
    row_block = lax.slice_in_dim(active, 0, tok_rows * lax.axis_size("tensor"), axis=0)
    ffn_out = (
        lax.psum_scatter(matmul(row_block, down_full), "tensor", scatter_dimension=0, tiled=True)
        + down_bias
    )
    second_sum = hidden + ffn_out
    layer_output = layer_norm(second_sum, norm2_gain, norm2_shift).astype(jnp.bfloat16)
    qkv_back, out_back, up_back, down_back = (qkv_full, out_full, up_full, down_full)
    unused_two, norm_two_back = jax.vjp(layer_norm, second_sum, norm2_gain, norm2_shift)
    grad_second, gain_two_grad, shift_two_grad = norm_two_back(cotangent.astype(jnp.float32))
    grad_ffn = grad_second.astype(jnp.bfloat16)
    down_bias_grad = jnp.sum(grad_ffn.astype(jnp.float32), axis=0)
    grad_ffn_all = lax.all_gather(grad_ffn, "tensor", axis=0, tiled=True)
    down_weight_grad = contract_rows(active, grad_ffn_all)
    grad_active = contract_cols(grad_ffn_all, down_back)
    unused_gelu, gelu_back = jax.vjp(gelu_exact, upper)
    grad_upper = gelu_back(grad_active)[0].astype(jnp.bfloat16)
    up_bias_grad = jnp.sum(grad_upper.astype(jnp.float32), axis=0)
    up_weight_grad = contract_rows(hidden_all, grad_upper)
    row_block = lax.slice_in_dim(grad_upper, 0, tok_rows * lax.axis_size("tensor"), axis=0)
    grad_hidden = grad_second + lax.psum_scatter(
        contract_cols(row_block, up_back), "tensor", scatter_dimension=0, tiled=True
    )
    unused_one, norm_one_back = jax.vjp(layer_norm, first_sum, norm1_gain, norm1_shift)
    grad_first, gain_one_grad, shift_one_grad = norm_one_back(grad_hidden)
    grad_attn = grad_first.astype(jnp.bfloat16)
    out_bias_grad = jnp.sum(grad_attn.astype(jnp.float32), axis=0)
    grad_attn_all = lax.all_gather(grad_attn, "tensor", axis=0, tiled=True)
    out_weight_grad = contract_rows(context_flat, grad_attn_all)
    grad_context = contract_cols(grad_attn_all, out_back).astype(jnp.bfloat16)

    def backward_seq(packed):
        seq_queries, seq_keys, seq_values, length, seq_grad, seq_totals = packed
        query_heads = seq_queries.reshape(LENGTH, head_count, HEAD_DIM)
        key_heads = seq_keys.reshape(LENGTH, head_count, HEAD_DIM)
        value_heads = seq_values.reshape(LENGTH, head_count, HEAD_DIM)
        usable = (positions < length)[None, None, :]
        key_grad = jnp.zeros((LENGTH, head_count, HEAD_DIM), jnp.float32)
        value_grad = jnp.zeros((LENGTH, head_count, HEAD_DIM), jnp.float32)
        query_blocks = []
        for block_start in range(0, LENGTH, block_rows):
            block_q = query_heads[block_start : block_start + block_rows]
            block_grad = seq_grad[block_start : block_start + block_rows].reshape(
                block_rows, head_count, HEAD_DIM
            )
            scores = (
                jnp.einsum("qhd,khd->hqk", block_q, key_heads, preferred_element_type=jnp.float32)
                * scaling
            )
            scores = jnp.where(usable, scores, NEGATIVE)
            chances = jnp.exp(scores - seq_totals[:, block_start : block_start + block_rows, None])
            weights = chances.astype(jnp.bfloat16)
            value_grad = value_grad + jnp.einsum(
                "hqk,qhd->khd", weights, block_grad, preferred_element_type=jnp.float32
            )
            grad_weights = jnp.einsum(
                "qhd,khd->hqk", block_grad, value_heads, preferred_element_type=jnp.float32
            )
            inner_sum = jnp.sum(grad_weights * chances, axis=-1, keepdims=True)
            grad_scores = (chances * (grad_weights - inner_sum)).astype(jnp.bfloat16)
            block_query_grad = (
                jnp.einsum(
                    "hqk,khd->qhd", grad_scores, key_heads, preferred_element_type=jnp.float32
                )
                * scaling
            )
            query_blocks.append(block_query_grad.reshape(block_rows, local_width))
            key_grad = (
                key_grad
                + jnp.einsum(
                    "hqk,qhd->khd", grad_scores, block_q, preferred_element_type=jnp.float32
                )
                * scaling
            )
        query_grad = jnp.concatenate(query_blocks, axis=0).astype(jnp.bfloat16)
        return (
            query_grad,
            key_grad.reshape(LENGTH, local_width).astype(jnp.bfloat16),
            value_grad.reshape(LENGTH, local_width).astype(jnp.bfloat16),
        )

    grad_shaped = grad_context.reshape(seq_count, LENGTH, local_width)
    query_grads, key_grads, value_grads = lax.map(
        backward_seq, (shaped[0], shaped[1], shaped[2], lengths, grad_shaped, log_totals)
    )
    query_grads = query_grads.reshape(seq_count * LENGTH, local_width)
    key_grads = key_grads.reshape(seq_count * LENGTH, local_width)
    value_grads = value_grads.reshape(seq_count * LENGTH, local_width)
    qv_bias_grad = jnp.stack(
        [
            jnp.sum(query_grads.astype(jnp.float32), axis=0),
            jnp.sum(value_grads.astype(jnp.float32), axis=0),
        ]
    )
    qkv_weight_grad = jnp.stack(
        [
            contract_rows(gathered, query_grads),
            contract_rows(gathered, key_grads),
            contract_rows(gathered, value_grads),
        ]
    )
    part_query = lax.slice_in_dim(query_grads, 0, lax.axis_size("tensor") * tok_rows, axis=0)
    input_grad = (
        grad_first
        + lax.psum_scatter(
            (
                contract_cols(part_query, qkv_back[0])
                + contract_cols(key_grads, qkv_back[1])
                + contract_cols(value_grads, qkv_back[2])
            ).astype(jnp.bfloat16),
            "tensor",
            scatter_dimension=0,
            tiled=True,
        ).astype(jnp.float32)
    ).astype(jnp.bfloat16)
    qkv_grad_own, out_grad_own, up_grad_own, down_grad_own = (
        lax.psum_scatter(qkv_weight_grad, "dp", scatter_dimension=1, tiled=True),
        lax.psum_scatter(out_weight_grad, "dp", scatter_dimension=1, tiled=True),
        lax.psum_scatter(up_weight_grad, "dp", scatter_dimension=0, tiled=True),
        lax.psum_scatter(down_weight_grad, "dp", scatter_dimension=1, tiled=True),
    )
    qv_bias_total, up_bias_total = lax.psum((qv_bias_grad, up_bias_grad), "dp")
    (
        out_bias_total,
        down_bias_total,
        gain_one_total,
        shift_one_total,
        gain_two_total,
        shift_two_total,
    ) = lax.psum(
        (
            out_bias_grad,
            down_bias_grad,
            gain_one_grad,
            shift_one_grad,
            gain_two_grad,
            shift_two_grad,
        ),
        ("dp", "tensor"),
    )
    return (
        layer_output,
        input_grad,
        qkv_grad_own,
        qv_bias_total,
        out_grad_own,
        out_bias_total,
        up_grad_own,
        up_bias_total,
        down_grad_own,
        down_bias_total,
        gain_one_total,
        shift_one_total,
        gain_two_total,
        shift_two_total,
    )


def solution(mesh):
    return jax.shard_map(
        per_device,
        mesh=mesh,
        in_specs=(
            P(("dp", "tensor"), None),
            P("dp"),
            P(None, "dp", "tensor"),
            P(None, "tensor"),
            P("tensor", "dp"),
            P(),
            P("dp", "tensor"),
            P("tensor"),
            P("tensor", "dp"),
            P(),
            P(),
            P(),
            P(),
            P(),
            P(("dp", "tensor"), None),
        ),
        out_specs=(
            P(("dp", "tensor"), None),
            P(("dp", "tensor"), None),
            P(None, "dp", "tensor"),
            P(None, "tensor"),
            P("tensor", "dp"),
            P(),
            P("dp", "tensor"),
            P("tensor"),
            P("tensor", "dp"),
            P(),
            P(),
            P(),
            P(),
            P(),
        ),
        check_vma=False,
    )
```

profile of v0, /device:TPU:0, one launch (start us, length us, event | category | flops | bytes accessed | tf_op | source)
XLA Modules:
  0.0 1038.2 jit_solution(9922317103957784277)
XLA Ops:
  10.1 49.1 %all_gather.26 = bf16[384,768]{0,1:T(8,128)(2,1)} all-gather(bf16[384,48]{0,1:T(8,128)(2,1)} %param.19), channel_id=1, replica_groups=mesh['dp'=16,'tensor'=2] {'dp'}, dimensions={1}, use_global_device_ids=true | all-gather | bytes 626688 | tf_op jit(solution)/shard_map/all_gather | solution.py:64
  59.2 25.9 %all-gather.10.cloned.1.call-done = bf16[3,768,384]{2,1,0:T(8,128)(2,1)} async-done(((bf16[3,48,384]{2,1,0:T(8,128)(2,1)}), bf16[3,768,384]{2,1,0:T(8,128)(2,1)}) %all-gather.10.cloned.1.call-update) | async-done | bytes 1769488 | tf_op jit(solution)/shard_map/all_gather | solution.py:63
  115.9 9.2 reduce-scatter.8.cloned.1.call-done
  129.2 62.5 %all-gather.14.cloned.1.call-done = bf16[768,1536]{1,0:T(8,128)(2,1)} async-done(((bf16[48,1536]{1,0:T(8,128)(2,1)}), bf16[768,1536]{1,0:T(8,128)(2,1)}) %all-gather.14.cloned.1.call-update) | async-done | bytes 2359312 | tf_op jit(solution)/shard_map/all_gather | solution.py:65
  191.6 10.7 %all-gather.12.cloned.1.call-done = bf16[1024,768]{1,0:T(8,128)(2,1)} async-done(((bf16[512,768]{1,0:T(8,128)(2,1)}), bf16[1024,768]{1,0:T(8,128)(2,1)}) %all-gather.12.cloned.1.call-update) | async-done | bytes 1572880 | tf_op jit(solution)/shard_map/all_gather | solution.py:117
  202.3 19.9 %multiply_convert_fusion.2 = (bf16[1024,1536]{1,0:T(8,128)(2,1)}, f32[1024,1536]{1,0:T(8,128)}, f32[1024,1536]{1,0:T(8,128)}) fusion(f32[1536]{0:T(1024)S(1)} %copy-done.44, bf16[1024,768]{1,0:T(8,128)(2,1)} %all-gather.12.cloned.1.call-done, bf16[768,1536]{1,0:T(8,128)(2,1)} %all-gather.14.cloned.1.call-done), kind=kOutput, calls=%fused_computation.24 | convolution fusion | flops 2519728128 | bytes 19666944 | tf_op jit(solution)/shard_map/dot_general | solution.py:23
  222.2 46.7 %all-gather.16.cloned.1.call-done = bf16[1536,768]{0,1:T(8,128)(2,1)} async-done(((bf16[1536,48]{0,1:T(8,128)(2,1)}), bf16[1536,768]{0,1:T(8,128)(2,1)}) %all-gather.16.cloned.1.call-update) | async-done | bytes 2359312 | tf_op jit(solution)/shard_map/all_gather | solution.py:66
  268.8 6.9 fusion.57
  275.8 9.8 reduce-scatter.10.cloned.1.call-done
  291.5 11.1 %all-gather.18.cloned.1.call-done = bf16[1024,768]{1,0:T(8,128)(2,1)} async-done(((bf16[512,768]{1,0:T(8,128)(2,1)}), bf16[1024,768]{1,0:T(8,128)(2,1)}) %all-gather.18.cloned.1.call-update) | async-done | bytes 1572880 | tf_op jit(solution)/shard_map/all_gather | solution.py:132
  302.5 10.9 %convert_reduce_fusion = (f32[1536]{0:T(1024)}, bf16[1024,1536]{1,0:T(8,128)(2,1)S(1)}) fusion(f32[1024,1536]{1,0:T(8,128)} %get-tuple-element.135, f32[1024,1536]{1,0:T(8,128)} %get-tuple-element.146, f32[1536]{0:T(1024)S(1)} %copy-done.44, bf16[1024,768]{1,0:T(8,128)(2,1)} %all-gather.18.cloned.1.call-done, ...), kind=kOutput, calls=%fused_computation.20 | convolution fusion | flops 2442656256 | bytes 19673088 | tf_op jit(solution)/shard_map/dot_general | solution.py:33
  319.5 12.2 %reduce-scatter.12.cloned.1.call-done = f32[512,768]{1,0:T(8,128)} async-done(((f32[1024,768]{1,0:T(8,128)}), f32[512,768]{1,0:T(8,128)}) %reduce-scatter.12.cloned.1.call-update) | async-done | bytes 1572880 | tf_op jit(solution)/shard_map/reduce_scatter | solution.py:140
  338.5 10.6 %all-gather.20.cloned.1.call-done = bf16[1024,768]{1,0:T(8,128)(2,1)} async-done(((bf16[512,768]{1,0:T(8,128)(2,1)}), bf16[1024,768]{1,0:T(8,128)(2,1)}) %all-gather.20.cloned.1.call-update) | async-done | bytes 1572880 | tf_op jit(solution)/shard_map/all_gather | solution.py:147
  351.4 6.4 fusion.59
  357.9 7.3 fusion.5
  365.1 18.9 %multiply_reduce_fusion.1 = (f32[6,512]{1,0:T(8,128)S(1)}, f32[6,512]{1,0:T(8,128)S(1)}, f32[6,512,1024]{2,1,0:T(8,128)}) fusion(f32[6,512]{1,0:T(8,128)S(1)} %get-tuple-element.151, f32[6,512,1024]{2,1,0:T(8,128)} %copy-done.1, pred[1024]{0:T(1024)(128)(4,1)S(1)} %iota_compare_fusion, f32[6,512,1024]{2,1,0:T(8,128)} %fusion.59, ...), kind=kOutput, calls=%fused_computation.4 | convolution fusion | flops 434104320 | bytes 51561472 | tf_op jit(solution)/shard_map/while/body/eval_jaxpr/qhd,khd->hqk/dot_general | solution.py:175
  384.1 17.3 %multiply_convert_fusion.1 = (bf16[6,512,1024]{2,1,0:T(8,128)(2,1)S(1)}, bf16[6,512,1024]{2,1,0:T(8,128)(2,1)S(1)}) fusion(f32[6,512,1024]{2,1,0:T(8,128)} %get-tuple-element.147, f32[6,512]{1,0:T(8,128)S(1)} %get-tuple-element.107, f32[6,512]{1,0:T(8,128)S(1)} %get-tuple-element.151, f32[6,512,1024]{2,1,0:T(8,128)} %copy-done.1, ...), kind=kLoop, calls=%fused_computation.3 | loop fusion | flops 37748736 | bytes 62964736 | tf_op jit(solution)/shard_map/while/body/eval_jaxpr/convert_element_type | solution.py:179
  405.0 7.2 convert_reduce_fusion.4
  449.8 43.9 %all-reduce.1 = (f32[768]{0:T(1024)}, f32[768]{0:T(1024)}, f32[768]{0:T(1024)}, f32[768]{0:T(1024)}, f32[768]{0:T(1024)}, /*index=5*/f32[768]{0:T(1024)}) all-reduce(f32[768]{0:T(1024)S(1)} %copy-done.30, f32[768]{0:T(1024)S(1)} %get-tuple-element.121, f32[768]{0:T(1024)S(1)} %copy-done.32, ...), channel_id=1, replica_groups=mesh['dp'=16,'tensor'=2] {'dp','tensor'}, use_global_device_ids=true, to_apply=%region_24.25 | all-reduce | flops 4608 | bytes 36864 | tf_op jit(solution)/shard_map/psum | solution.py:249
  494.0 76.4 %all-reduce.2 = (f32[2,384]{1,0:T(2,128)}, f32[1536]{0:T(1024)}) all-reduce(f32[2,384]{1,0:T(2,128)S(1)} %pad_maximum_fusion.7, f32[1536]{0:T(1024)S(1)} %copy-done.34), channel_id=1, replica_groups=mesh['dp'=16,'tensor'=2] {'dp'}, use_global_device_ids=true, to_apply=%region_21.22 | all-reduce | flops 2304 | bytes 18432 | tf_op jit(solution)/shard_map/psum | solution.py:241
  572.7 45.6 %all-reduce.5.cloned.1.call-done = f32[3,768,384]{2,0,1:T(4,128)} async-done(((f32[3,768,384]{2,0,1:T(4,128)}), f32[3,768,384]{2,0,1:T(4,128)}) %all-reduce.5.cloned.1.call-update) | async-done | bytes 3538960
  620.1 141.2 %reduce-scatter.20.cloned.1.call-done = f32[1536,48]{0,1:T(8,128)} async-done(((f32[1536,768]{0,1:T(8,128)}), f32[1536,48]{0,1:T(8,128)}) %reduce-scatter.20.cloned.1.call-update) | async-done | bytes 294928 | tf_op jit(solution)/shard_map/reduce_scatter | solution.py:239
  761.2 141.7 %reduce-scatter.18.cloned.1.call-done = f32[48,1536]{1,0:T(8,128)} async-done(((f32[768,1536]{1,0:T(8,128)}), f32[48,1536]{1,0:T(8,128)}) %reduce-scatter.18.cloned.1.call-update) | async-done | bytes 294928 | tf_op jit(solution)/shard_map/reduce_scatter | solution.py:238
  902.9 128.6 %reduce-scatter.16.cloned.1.call-done = f32[384,48]{0,1:T(8,128)} async-done(((f32[384,768]{0,1:T(8,128)}), f32[384,48]{0,1:T(8,128)}) %reduce-scatter.16.cloned.1.call-update) | async-done | bytes 73744 | tf_op jit(solution)/shard_map/reduce_scatter | solution.py:237
  (184 shorter events, 102.2 us)
Async XLA Ops:
  7.2 52.0 %all-gather.8.cloned.1.call-start = ((), (), s32[]{:S(2)}) async-start(), calls=%async_computation.7 | async-start | bytes 2359296 | tf_op jit(solution)/shard_map/all_gather | solution.py:68
  7.9 77.2 %all-gather.10.cloned.1.call-start = ((), (), s32[]{:S(2)}) async-start(), calls=%async_computation.8 | async-start | bytes 1880064 | tf_op jit(solution)/shard_map/all_gather | solution.py:63
  8.7 116.4 %reduce-scatter.8.cloned.1.call-start = ((), (), s32[]{:S(2)}) async-start(), calls=%async_computation.9 | async-start | bytes 4718592 | tf_op jit(solution)/shard_map/reduce_scatter | solution.py:111
  59.2 28.3 %copy-start.40 = (bf16[1024,768]{1,0:T(8,128)(2,1)S(1)}, bf16[1024,768]{1,0:T(8,128)(2,1)}, u32[]{:S(2)}) copy-start(bf16[1024,768]{1,0:T(8,128)(2,1)} %all-gather.8.cloned.1.call-done) | copy-start | bytes 4718596
  115.3 76.3 %all-gather.14.cloned.1.call-start = ((), (), s32[]{:S(2)}) async-start(), calls=%async_computation.11 | async-start | bytes 2506752 | tf_op jit(solution)/shard_map/all_gather | solution.py:65
  115.9 86.4 %all-gather.12.cloned.1.call-start = ((), (), s32[]{:S(2)}) async-start(), calls=%async_computation.10 | async-start | bytes 2359296 | tf_op jit(solution)/shard_map/all_gather | solution.py:117
  126.8 75.5 %copy-start.44 = (f32[1536]{0:T(1024)S(1)}, f32[1536]{0:T(1024)}, u32[]{:S(2)}) copy-start(f32[1536]{0:T(1024)} %param.22) | copy-start | bytes 18436
  128.4 140.5 %all-gather.16.cloned.1.call-start = ((), (), s32[]{:S(2)}) async-start(), calls=%async_computation.12 | async-start | bytes 2506752 | tf_op jit(solution)/shard_map/all_gather | solution.py:66
  128.9 156.7 %reduce-scatter.10.cloned.1.call-start = ((), (), s32[]{:S(2)}) async-start(), calls=%async_computation.13 | async-start | bytes 4718592 | tf_op jit(solution)/shard_map/reduce_scatter | solution.py:122
  275.8 26.8 %all-gather.18.cloned.1.call-start = ((), (), s32[]{:S(2)}) async-start(), calls=%async_computation.14 | async-start | bytes 2359296 | tf_op jit(solution)/shard_map/all_gather | solution.py:132
  291.4 40.3 %reduce-scatter.12.cloned.1.call-start = ((), (), s32[]{:S(2)}) async-start(), calls=%async_computation.15 | async-start | bytes 4718592 | tf_op jit(solution)/shard_map/reduce_scatter | solution.py:140
  319.5 29.7 %all-gather.20.cloned.1.call-start = ((), (), s32[]{:S(2)}) async-start(), calls=%async_computation.16 | async-start | bytes 2359296 | tf_op jit(solution)/shard_map/all_gather | solution.py:147
  338.0 232.5 %reduce-scatter.14.cloned.1.call-start = ((), (), s32[]{:S(2)}) async-start(), calls=%async_computation.17 | async-start | bytes 2359296 | tf_op jit(solution)/shard_map/reduce_scatter | solution.py:224
  384.1 17.3 %copy-start.5 = (bf16[1024,384]{0,1:T(8,128)(2,1)S(1)}, bf16[1024,384]{0,1:T(8,128)(2,1)}, u32[]{:S(2)}) copy-start(bf16[1024,384]{0,1:T(8,128)(2,1)} %copy-done.4) | copy-start | bytes 2359300
  403.5 16.7 %copy-start.10 = (bf16[6,64,512]{2,1,0:T(8,128)(2,1)}, bf16[6,64,512]{2,1,0:T(8,128)(2,1)S(1)}, u32[]{:S(2)}) copy-start(bf16[6,64,512]{2,1,0:T(8,128)(2,1)S(1)} %fusion.27) | copy-start | bytes 1179652
  420.2 198.2 %all-reduce.5.cloned.1.call-start = ((), (), s32[]{:S(2)}) async-start(), calls=%async_computation.21 | async-start | bytes 9437184
  428.4 332.8 %reduce-scatter.20.cloned.1.call-start = ((), (), s32[]{:S(2)}) async-start(), calls=%async_computation.20 | async-start | bytes 5013504 | tf_op jit(solution)/shard_map/reduce_scatter | solution.py:239
  436.2 466.7 %reduce-scatter.18.cloned.1.call-start = ((), (), s32[]{:S(2)}) async-start(), calls=%async_computation.19 | async-start | bytes 5013504 | tf_op jit(solution)/shard_map/reduce_scatter | solution.py:238
  443.9 49.8 %copy-start.36 = (f32[6,64]{1,0:T(8,128)S(1)}, f32[6,64]{1,0:T(8,128)}, u32[]{:S(2)}) copy-start(f32[6,64]{1,0:T(8,128)} %get-tuple-element.148) | copy-start | bytes 4612
  443.9 49.9 %copy-start.11 = (bf16[6,64,512]{2,1,0:T(8,128)(2,1)S(1)}, bf16[6,64,512]{2,1,0:T(8,128)(2,1)}, u32[]{:S(2)}) copy-start(bf16[6,64,512]{2,1,0:T(8,128)(2,1)} %copy-done.10) | copy-start | bytes 1179652
  444.0 49.8 %copy-start.13 = (bf16[6,64,512]{2,1,0:T(8,128)(2,1)S(1)}, bf16[6,64,512]{2,1,0:T(8,128)(2,1)}, u32[]{:S(2)}) copy-start(bf16[6,64,512]{2,1,0:T(8,128)(2,1)} %copy-done.12) | copy-start | bytes 1179652
  444.0 50.0 %copy-start.34 = (f32[1536]{0:T(1024)S(1)}, f32[1536]{0:T(1024)}, u32[]{:S(2)}) copy-start(f32[1536]{0:T(1024)} %get-tuple-element.125) | copy-start | bytes 18436
  444.0 126.5 %copy-start.3 = (f32[512,768]{1,0:T(8,128)S(1)}, f32[512,768]{1,0:T(8,128)}, u32[]{:S(2)}) copy-start(f32[512,768]{1,0:T(8,128)} %copy-done.2) | copy-start | bytes 4718596
  444.0 587.5 %reduce-scatter.16.cloned.1.call-start = ((), (), s32[]{:S(2)}) async-start(), calls=%async_computation.18 | async-start | bytes 1253376 | tf_op jit(solution)/shard_map/reduce_scatter | solution.py:237
  (38 other events, 224.5 us)
Sparse Core Ops, SparseCore 0:
  9.6 12.4 all-gather.7
  24.8 60.2 all-gather.9
  115.4 9.6 reduce-scatter.7
  128.1 63.4 all-gather.13
  193.7 8.6 all-gather.11
  205.3 63.4 all-gather.15
  275.9 9.7 reduce-scatter.9
  291.5 10.9 all-gather.17
  319.6 12.0 reduce-scatter.11
  338.1 10.9 all-gather.19
  420.3 10.2 reduce-scatter.13
  436.1 182.1 all-reduce.4
  624.9 136.2 reduce-scatter.19
  766.8 136.0 reduce-scatter.17
  908.8 122.6 reduce-scatter.15
where the time goes:
time: 1050 us; the launch traced here: 1040 us
  waiting for transfers between devices  658 us (63%)
  blocking collectives  169 us (16%)
  matrix products  138 us (13%)
  other arithmetic  39.6 us (4%)
  between operations  16.1 us (2%)
  local copies, waits for them, and re-layouts  15.8 us (2%)
    reduce_scatter x1, waiting for transfers between devices, per_device(): lax.psum_scatter(up_weight_grad, 'dp', scatter_dimension=0, tiled=True)  142 us
    reduce_scatter x1, waiting for transfers between devices, per_device(): lax.psum_scatter(down_weight_grad, 'dp', scatter_dimension=1, tiled=True)  141 us
    reduce_scatter x1, waiting for transfers between devices, per_device(): lax.psum_scatter(out_weight_grad, 'dp', scatter_dimension=1, tiled=True)  129 us
    psum x1, blocking collectives, per_device(): qv_bias_total, up_bias_total = lax.psum((qv_bias_grad, up_bias_grad), 'dp')  76.4 us
    all_gather x1, waiting for transfers between devices, per_device(): lax.all_gather(up_weight, 'dp', axis=0, tiled=True)  62.5 us
    all_gather x1, blocking collectives, per_device(): lax.all_gather(out_weight, 'dp', axis=1, tiled=True)  49.1 us
    unnamed x16, waiting for transfers between devices  48.2 us
    all_gather x1, waiting for transfers between devices, per_device(): lax.all_gather(down_weight, 'dp', axis=1, tiled=True)  46.7 us
  transfers between devices with their start and end apart: 15, of which 13 were waited for; matrix products, arithmetic and copies ran while one was open for 5% of the time, Pallas kernels for 0%

commit v1 on v0

--- a/solution.py
+++ b/solution.py
@@ -61,7 +61,9 @@
     positions = jnp.arange(LENGTH)
     qkv_full, out_full, up_full, down_full = (
         lax.all_gather(qkv_weight, "dp", axis=1, tiled=True),
-        lax.all_gather(out_weight, "dp", axis=1, tiled=True),
+        jnp.concatenate(
+            lax.all_to_all(jnp.stack([out_weight] * lax.axis_size("dp")), "dp", 0, 0), axis=1
+        ),
         lax.all_gather(up_weight, "dp", axis=0, tiled=True),
         lax.all_gather(down_weight, "dp", axis=1, tiled=True),
     )

time: 1050 us -> 1050 us (level)
  blocking collectives: 169 us -> 120 us
  waiting for transfers between devices: 658 us -> 697 us
    all_gather x1 -> x0, blocking collectives: 49.1 us -> none  [per_device(): lax.all_gather(out_weight, 'dp', axis=1, tiled=True)]
    all_gather x1, waiting for transfers between devices: 25.9 us -> 62.8 us  [per_device(): lax.all_gather(qkv_weight, 'dp', axis=1, tiled=True)]
  transfers between devices with their start and end apart: 15 -> 16, of which waited for: 13 -> 14; matrix products, arithmetic and copies ran while one was open for 5% -> 8% of each run, Pallas kernels for 0% -> 0%
where the time goes in v1:
time: 1050 us; the launch traced here: 1040 us
  waiting for transfers between devices  697 us (66%)
  matrix products  139 us (13%)
  blocking collectives  120 us (11%)
  other arithmetic  39.6 us (4%)
  local copies, waits for them, and re-layouts  16.7 us (2%)
  between operations  16.2 us (2%)
    reduce_scatter x1, waiting for transfers between devices, per_device(): lax.psum_scatter(up_weight_grad, 'dp', scatter_dimension=0, tiled=True)  142 us
    reduce_scatter x1, waiting for transfers between devices, per_device(): lax.psum_scatter(down_weight_grad, 'dp', scatter_dimension=1, tiled=True)  141 us
    reduce_scatter x1, waiting for transfers between devices, per_device(): lax.psum_scatter(out_weight_grad, 'dp', scatter_dimension=1, tiled=True)  129 us
    psum x1, blocking collectives, per_device(): qv_bias_total, up_bias_total = lax.psum((qv_bias_grad, up_bias_grad), 'dp')  76.4 us
    all_gather x1, waiting for transfers between devices, per_device(): lax.all_gather(qkv_weight, 'dp', axis=1, tiled=True)  62.8 us
    all_gather x1, waiting for transfers between devices, per_device(): lax.all_gather(up_weight, 'dp', axis=0, tiled=True)  62.5 us
    unnamed x16, waiting for transfers between devices  48.2 us
    all_gather x1, waiting for transfers between devices, per_device(): lax.all_gather(down_weight, 'dp', axis=1, tiled=True)  46.7 us
  transfers between devices with their start and end apart: 16, of which 14 were waited for; matrix products, arithmetic and copies ran while one was open for 8% of the time, Pallas kernels for 0%

profile of v1, /device:TPU:0, one launch (start us, length us, event | category | flops | bytes accessed | tf_op | source)
XLA Modules:
  0.0 1038.6 jit_solution(8155375425013341497)
XLA Ops:
  10.3 8.4 all-to-all-start
  22.1 62.8 %all-gather.10.cloned.1.call-done = bf16[3,768,384]{2,1,0:T(8,128)(2,1)} async-done(((bf16[3,48,384]{2,1,0:T(8,128)(2,1)}), bf16[3,768,384]{2,1,0:T(8,128)(2,1)}) %all-gather.10.cloned.1.call-update) | async-done | bytes 1769488 | tf_op jit(solution)/shard_map/all_gather | solution.py:63
  116.2 9.2 reduce-scatter.8.cloned.1.call-done
  129.5 62.5 %all-gather.14.cloned.1.call-done = bf16[768,1536]{1,0:T(8,128)(2,1)} async-done(((bf16[48,1536]{1,0:T(8,128)(2,1)}), bf16[768,1536]{1,0:T(8,128)(2,1)}) %all-gather.14.cloned.1.call-update) | async-done | bytes 2359312 | tf_op jit(solution)/shard_map/all_gather | solution.py:67
  191.9 10.7 %all-gather.12.cloned.1.call-done = bf16[1024,768]{1,0:T(8,128)(2,1)} async-done(((bf16[512,768]{1,0:T(8,128)(2,1)}), bf16[1024,768]{1,0:T(8,128)(2,1)}) %all-gather.12.cloned.1.call-update) | async-done | bytes 1572880 | tf_op jit(solution)/shard_map/all_gather | solution.py:119
  202.6 19.9 %multiply_convert_fusion.2 = (bf16[1024,1536]{1,0:T(8,128)(2,1)}, f32[1024,1536]{1,0:T(8,128)}, f32[1024,1536]{1,0:T(8,128)}) fusion(f32[1536]{0:T(1024)S(1)} %copy-done.42, bf16[1024,768]{1,0:T(8,128)(2,1)} %all-gather.12.cloned.1.call-done, bf16[768,1536]{1,0:T(8,128)(2,1)} %all-gather.14.cloned.1.call-done), kind=kOutput, calls=%fused_computation.24 | convolution fusion | flops 2519728128 | bytes 19666944 | tf_op jit(solution)/shard_map/dot_general | solution.py:23
  222.5 46.7 %all-gather.16.cloned.1.call-done = bf16[1536,768]{0,1:T(8,128)(2,1)} async-done(((bf16[1536,48]{0,1:T(8,128)(2,1)}), bf16[1536,768]{0,1:T(8,128)(2,1)}) %all-gather.16.cloned.1.call-update) | async-done | bytes 2359312 | tf_op jit(solution)/shard_map/all_gather | solution.py:68
  269.1 6.9 fusion.57
  276.1 9.8 reduce-scatter.10.cloned.1.call-done
  291.8 11.1 %all-gather.18.cloned.1.call-done = bf16[1024,768]{1,0:T(8,128)(2,1)} async-done(((bf16[512,768]{1,0:T(8,128)(2,1)}), bf16[1024,768]{1,0:T(8,128)(2,1)}) %all-gather.18.cloned.1.call-update) | async-done | bytes 1572880 | tf_op jit(solution)/shard_map/all_gather | solution.py:134
  302.9 10.9 %convert_reduce_fusion = (f32[1536]{0:T(1024)}, bf16[1024,1536]{1,0:T(8,128)(2,1)S(1)}) fusion(f32[1024,1536]{1,0:T(8,128)} %get-tuple-element.149, f32[1024,1536]{1,0:T(8,128)} %get-tuple-element.160, f32[1536]{0:T(1024)S(1)} %copy-done.42, bf16[1024,768]{1,0:T(8,128)(2,1)} %all-gather.18.cloned.1.call-done, ...), kind=kOutput, calls=%fused_computation.20 | convolution fusion | flops 2442656256 | bytes 19673088 | tf_op jit(solution)/shard_map/dot_general | solution.py:33
  319.8 12.2 %reduce-scatter.12.cloned.1.call-done = f32[512,768]{1,0:T(8,128)} async-done(((f32[1024,768]{1,0:T(8,128)}), f32[512,768]{1,0:T(8,128)}) %reduce-scatter.12.cloned.1.call-update) | async-done | bytes 1572880 | tf_op jit(solution)/shard_map/reduce_scatter | solution.py:142
  338.8 10.6 %all-gather.20.cloned.1.call-done = bf16[1024,768]{1,0:T(8,128)(2,1)} async-done(((bf16[512,768]{1,0:T(8,128)(2,1)}), bf16[1024,768]{1,0:T(8,128)(2,1)}) %all-gather.20.cloned.1.call-update) | async-done | bytes 1572880 | tf_op jit(solution)/shard_map/all_gather | solution.py:149
  351.9 6.4 fusion.59
  358.3 7.3 fusion.5
  365.6 18.9 %multiply_reduce_fusion.1 = (f32[6,512]{1,0:T(8,128)S(1)}, f32[6,512]{1,0:T(8,128)S(1)}, f32[6,512,1024]{2,1,0:T(8,128)}) fusion(f32[6,512]{1,0:T(8,128)S(1)} %get-tuple-element.165, f32[6,512,1024]{2,1,0:T(8,128)} %copy-done.1, pred[1024]{0:T(1024)(128)(4,1)S(1)} %iota_compare_fusion, f32[6,512,1024]{2,1,0:T(8,128)} %fusion.59, ...), kind=kOutput, calls=%fused_computation.4 | convolution fusion | flops 434104320 | bytes 51561472 | tf_op jit(solution)/shard_map/while/body/eval_jaxpr/qhd,khd->hqk/dot_general | solution.py:177
  384.5 17.3 %multiply_convert_fusion.1 = (bf16[6,512,1024]{2,1,0:T(8,128)(2,1)S(1)}, bf16[6,512,1024]{2,1,0:T(8,128)(2,1)S(1)}) fusion(f32[6,512,1024]{2,1,0:T(8,128)} %get-tuple-element.161, f32[6,512]{1,0:T(8,128)S(1)} %get-tuple-element.121, f32[6,512]{1,0:T(8,128)S(1)} %get-tuple-element.165, f32[6,512,1024]{2,1,0:T(8,128)} %copy-done.1, ...), kind=kLoop, calls=%fused_computation.3 | loop fusion | flops 37748736 | bytes 62964736 | tf_op jit(solution)/shard_map/while/body/eval_jaxpr/convert_element_type | solution.py:181
  405.5 7.2 convert_reduce_fusion.4
  450.2 43.9 %all-reduce.1 = (f32[768]{0:T(1024)}, f32[768]{0:T(1024)}, f32[768]{0:T(1024)}, f32[768]{0:T(1024)}, f32[768]{0:T(1024)}, /*index=5*/f32[768]{0:T(1024)}) all-reduce(f32[768]{0:T(1024)S(1)} %copy-done.28, f32[768]{0:T(1024)S(1)} %get-tuple-element.135, f32[768]{0:T(1024)S(1)} %copy-done.30, ...), channel_id=1, replica_groups=mesh['dp'=16,'tensor'=2] {'dp','tensor'}, use_global_device_ids=true, to_apply=%region_24.25 | all-reduce | flops 4608 | bytes 36864 | tf_op jit(solution)/shard_map/psum | solution.py:251
  494.5 76.4 %all-reduce.2 = (f32[2,384]{1,0:T(2,128)}, f32[1536]{0:T(1024)}) all-reduce(f32[2,384]{1,0:T(2,128)S(1)} %pad_maximum_fusion.7, f32[1536]{0:T(1024)S(1)} %copy-done.32), channel_id=1, replica_groups=mesh['dp'=16,'tensor'=2] {'dp'}, use_global_device_ids=true, to_apply=%region_21.22 | all-reduce | flops 2304 | bytes 18432 | tf_op jit(solution)/shard_map/psum | solution.py:243
  573.1 45.6 %all-reduce.5.cloned.1.call-done = f32[3,768,384]{2,0,1:T(4,128)} async-done(((f32[3,768,384]{2,0,1:T(4,128)}), f32[3,768,384]{2,0,1:T(4,128)}) %all-reduce.5.cloned.1.call-update) | async-done | bytes 3538960
  620.4 141.2 %reduce-scatter.20.cloned.1.call-done = f32[1536,48]{0,1:T(8,128)} async-done(((f32[1536,768]{0,1:T(8,128)}), f32[1536,48]{0,1:T(8,128)}) %reduce-scatter.20.cloned.1.call-update) | async-done | bytes 294928 | tf_op jit(solution)/shard_map/reduce_scatter | solution.py:241
  761.6 141.7 %reduce-scatter.18.cloned.1.call-done = f32[48,1536]{1,0:T(8,128)} async-done(((f32[768,1536]{1,0:T(8,128)}), f32[48,1536]{1,0:T(8,128)}) %reduce-scatter.18.cloned.1.call-update) | async-done | bytes 294928 | tf_op jit(solution)/shard_map/reduce_scatter | solution.py:240
  903.2 128.6 %reduce-scatter.16.cloned.1.call-done = f32[384,48]{0,1:T(8,128)} async-done(((f32[384,768]{0,1:T(8,128)}), f32[384,48]{0,1:T(8,128)}) %reduce-scatter.16.cloned.1.call-update) | async-done | bytes 73744 | tf_op jit(solution)/shard_map/reduce_scatter | solution.py:239
  (182 shorter events, 106.4 us)
Async XLA Ops:
  7.2 14.9 %all-gather.8.cloned.1.call-start = ((), (), s32[]{:S(2)}) async-start(), calls=%async_computation.8 | async-start | bytes 2359296 | tf_op jit(solution)/shard_map/all_gather | solution.py:70
  7.9 77.0 %all-gather.10.cloned.1.call-start = ((), (), s32[]{:S(2)}) async-start(), calls=%async_computation.9 | async-start | bytes 1880064 | tf_op jit(solution)/shard_map/all_gather | solution.py:63
  10.3 101.3 %all-to-all-start = ((bf16[16,384,48]{1,2,0:T(8,128)(2,1)}), bf16[16,384,48]{1,2,0:T(8,128)(2,1)}, u32[]{:S(2)}, u32[]{:S(2)}) async-start(bf16[16,384,48]{1,2,0:T(8,128)(2,1)} %stack.16), calls=%async_computation | async-start | bytes 1179648 | tf_op jit(solution)/shard_map/all_to_all | solution.py:65
  18.7 106.7 %reduce-scatter.8.cloned.1.call-start = ((), (), s32[]{:S(2)}) async-start(), calls=%async_computation.10 | async-start | bytes 4718592 | tf_op jit(solution)/shard_map/reduce_scatter | solution.py:113
  22.1 65.3 %copy-start.38 = (bf16[1024,768]{1,0:T(8,128)(2,1)S(1)}, bf16[1024,768]{1,0:T(8,128)(2,1)}, u32[]{:S(2)}) copy-start(bf16[1024,768]{1,0:T(8,128)(2,1)} %all-gather.8.cloned.1.call-done) | copy-start | bytes 4718596
  115.6 76.3 %all-gather.14.cloned.1.call-start = ((), (), s32[]{:S(2)}) async-start(), calls=%async_computation.12 | async-start | bytes 2506752 | tf_op jit(solution)/shard_map/all_gather | solution.py:67
  116.2 86.4 %all-gather.12.cloned.1.call-start = ((), (), s32[]{:S(2)}) async-start(), calls=%async_computation.11 | async-start | bytes 2359296 | tf_op jit(solution)/shard_map/all_gather | solution.py:119
  127.1 75.5 %copy-start.42 = (f32[1536]{0:T(1024)S(1)}, f32[1536]{0:T(1024)}, u32[]{:S(2)}) copy-start(f32[1536]{0:T(1024)} %param.22) | copy-start | bytes 18436
  128.6 140.5 %all-gather.16.cloned.1.call-start = ((), (), s32[]{:S(2)}) async-start(), calls=%async_computation.13 | async-start | bytes 2506752 | tf_op jit(solution)/shard_map/all_gather | solution.py:68
  129.2 156.7 %reduce-scatter.10.cloned.1.call-start = ((), (), s32[]{:S(2)}) async-start(), calls=%async_computation.14 | async-start | bytes 4718592 | tf_op jit(solution)/shard_map/reduce_scatter | solution.py:124
  276.1 26.8 %all-gather.18.cloned.1.call-start = ((), (), s32[]{:S(2)}) async-start(), calls=%async_computation.15 | async-start | bytes 2359296 | tf_op jit(solution)/shard_map/all_gather | solution.py:134
  291.7 40.3 %reduce-scatter.12.cloned.1.call-start = ((), (), s32[]{:S(2)}) async-start(), calls=%async_computation.16 | async-start | bytes 4718592 | tf_op jit(solution)/shard_map/reduce_scatter | solution.py:142
  319.8 29.7 %all-gather.20.cloned.1.call-start = ((), (), s32[]{:S(2)}) async-start(), calls=%async_computation.17 | async-start | bytes 2359296 | tf_op jit(solution)/shard_map/all_gather | solution.py:149
  338.4 232.5 %reduce-scatter.14.cloned.1.call-start = ((), (), s32[]{:S(2)}) async-start(), calls=%async_computation.18 | async-start | bytes 2359296 | tf_op jit(solution)/shard_map/reduce_scatter | solution.py:226
  384.5 17.3 %copy-start.5 = (bf16[1024,384]{0,1:T(8,128)(2,1)S(1)}, bf16[1024,384]{0,1:T(8,128)(2,1)}, u32[]{:S(2)}) copy-start(bf16[1024,384]{0,1:T(8,128)(2,1)} %copy-done.4) | copy-start | bytes 2359300
  420.6 198.1 %all-reduce.5.cloned.1.call-start = ((), (), s32[]{:S(2)}) async-start(), calls=%async_computation.22 | async-start | bytes 9437184
  428.9 332.7 %reduce-scatter.20.cloned.1.call-start = ((), (), s32[]{:S(2)}) async-start(), calls=%async_computation.21 | async-start | bytes 5013504 | tf_op jit(solution)/shard_map/reduce_scatter | solution.py:241
  436.7 466.6 %reduce-scatter.18.cloned.1.call-start = ((), (), s32[]{:S(2)}) async-start(), calls=%async_computation.20 | async-start | bytes 5013504 | tf_op jit(solution)/shard_map/reduce_scatter | solution.py:240
  444.4 49.8 %copy-start.34 = (f32[6,64]{1,0:T(8,128)S(1)}, f32[6,64]{1,0:T(8,128)}, u32[]{:S(2)}) copy-start(f32[6,64]{1,0:T(8,128)} %get-tuple-element.162) | copy-start | bytes 4612
  444.4 49.9 %copy-start.11 = (bf16[6,64,512]{2,1,0:T(8,128)(2,1)S(1)}, bf16[6,64,512]{2,1,0:T(8,128)(2,1)}, u32[]{:S(2)}) copy-start(bf16[6,64,512]{2,1,0:T(8,128)(2,1)} %copy-done.10) | copy-start | bytes 1179652
  444.4 49.8 %copy-start.13 = (bf16[6,64,512]{2,1,0:T(8,128)(2,1)S(1)}, bf16[6,64,512]{2,1,0:T(8,128)(2,1)}, u32[]{:S(2)}) copy-start(bf16[6,64,512]{2,1,0:T(8,128)(2,1)} %copy-done.12) | copy-start | bytes 1179652
  444.4 50.0 %copy-start.32 = (f32[1536]{0:T(1024)S(1)}, f32[1536]{0:T(1024)}, u32[]{:S(2)}) copy-start(f32[1536]{0:T(1024)} %get-tuple-element.139) | copy-start | bytes 18436
  444.4 126.5 %copy-start.3 = (f32[512,768]{1,0:T(8,128)S(1)}, f32[512,768]{1,0:T(8,128)}, u32[]{:S(2)}) copy-start(f32[512,768]{1,0:T(8,128)} %copy-done.2) | copy-start | bytes 4718596
  444.4 587.4 %reduce-scatter.16.cloned.1.call-start = ((), (), s32[]{:S(2)}) async-start(), calls=%async_computation.19 | async-start | bytes 1253376 | tf_op jit(solution)/shard_map/reduce_scatter | solution.py:239
  (37 other events, 227.9 us)
Sparse Core Ops, SparseCore 0:
  9.6 12.4 all-gather.7
  24.8 60.1 all-gather.9
  115.7 9.6 reduce-scatter.7
  128.4 63.4 all-gather.13
  194.0 8.6 all-gather.11
  205.6 63.4 all-gather.15
  276.2 9.7 reduce-scatter.9
  291.9 10.9 all-gather.17
  319.9 12.0 reduce-scatter.11
  338.5 10.9 all-gather.19
  420.7 10.2 reduce-scatter.13
  436.6 182.0 all-reduce.4
  625.3 136.2 reduce-scatter.19
  767.2 136.0 reduce-scatter.17
  909.1 122.6 reduce-scatter.15
